TPU v7x, 32 devices: a whole 2x2x4 slice. The times are simulated.
32 devices in a mesh: seq: 16 (over z, x, core), ch: 2 (over y).
Axes of the slice: x: 2, y: 2, z: 4, core: 2. Of those that a mesh axis runs over, the one named last changes fastest.
Arguments:
- inputs: bfloat16 [256, 8192], P('ch', 'seq'), may hold values from -6 to 6
- proj_weight: bfloat16 [3, 256, 256], P(None, 'ch'), may hold values from -0.5 to 0.5
- short_taps: float32 [256, 3, 3], P('ch'), may hold values from -3 to 3
- skip_gain: float32 [256, 2], P('ch'), may hold values from -1 to 1
- filters: float32 [2, 256, 8192], P(None, 'ch', 'seq'), may hold values from -1 to 1
- out_weight: bfloat16 [256, 256], P('ch'), may hold values from -0.5 to 0.5
Outputs:
- outputs: bfloat16 [256, 8192], P('ch', 'seq')
All inputs are finite; a program needn't handle non-finite values.
Results may differ from a plain program's by a relative error of at most 0.007.
Values may be sent and summed in bfloat16 or wider, within the bound.
A program may use at most 64 MiB of HBM per device.

v0:
```python
import functools
import math

import jax
import jax.numpy as jnp
from jax import lax
from jax.experimental import pallas as pl
from jax.experimental.pallas import tpu as pltpu
from jax.sharding import PartitionSpec as P

highest = lax.Precision.HIGHEST


def passed_along(shard, axis, by):
    size = lax.axis_size(axis)
    pairs = [(i, i + by) for i in range(size) if 0 <= i + by < size]
    return lax.ppermute(shard, axis, pairs)


def complex_product(left, right):
    return jnp.stack(
        [left[0] * right[0] - left[1] * right[1], left[0] * right[1] + left[1] * right[0]]
    )


def twiddle(spectrum, first_row, total, undo):
    length = spectrum.shape[-1]
    column = jnp.arange(length, dtype=jnp.int32)
    row_index = first_row + jnp.arange(2, dtype=jnp.int32)
    angle = (
        2.0 * math.pi / total * (row_index[:, None] * column[None, :] % total).astype(jnp.float32)
    )
    cosine = jnp.cos(angle)
    sine = jnp.sin(angle)
    real_part = spectrum[0]
    imag_part = spectrum[1]
    if undo:
        return jnp.stack(
            [real_part * cosine - imag_part * sine, real_part * sine + imag_part * cosine]
        )
    return jnp.stack([real_part * cosine + imag_part * sine, imag_part * cosine - real_part * sine])


def local_dft(spectrum, undo):
    length = spectrum.shape[-1]
    width = min(128, length)
    column = jnp.arange(length, dtype=jnp.int32)
    blocks = []
    for block in range(length // width):
        target = block * width + jnp.arange(width, dtype=jnp.int32)
        angle = (
            2.0
            * math.pi
            / length
            * (column[:, None] * target[None, :] % length).astype(jnp.float32)
        )
        table = jnp.stack([jnp.cos(angle), jnp.sin(angle)])
        products = jnp.einsum("xrem,ymd->xyred", spectrum, table, precision=highest)
        if undo:
            blocks.append(
                jnp.stack([products[0, 0] - products[1, 1], products[0, 1] + products[1, 0]])
            )
        else:
            blocks.append(
                jnp.stack([products[0, 0] + products[1, 1], products[1, 0] - products[0, 1]])
            )
    return jnp.concatenate(blocks, axis=-1)


def forward(signal):
    count = lax.axis_size("seq")
    device = lax.axis_index("seq")
    length = signal.shape[-1]
    total = 2 * count * length
    spread = lax.all_to_all(signal[:, None, :], "seq", split_axis=2, concat_axis=1, tiled=True)
    source = jnp.arange(count, dtype=jnp.int32)
    target = jnp.arange(2 * count, dtype=jnp.int32)
    angle = math.pi / count * (target[:, None] * source[None, :] % (2 * count)).astype(jnp.float32)
    table = jnp.stack([jnp.cos(angle), -jnp.sin(angle)])
    summed = jnp.einsum("xka,rab->xrkb", table, spread, precision=highest)
    state = lax.all_to_all(summed, "seq", split_axis=2, concat_axis=3, tiled=True)
    first_row = 2 * device
    return local_dft(twiddle(state, first_row, total, False), False)


def inverse(spectrum):
    count = lax.axis_size("seq")
    device = lax.axis_index("seq")
    length = spectrum.shape[-1]
    total = 2 * count * length
    first_row = 2 * device
    state = twiddle(local_dft(spectrum, True), first_row, total, True)
    spread = lax.all_to_all(state, "seq", split_axis=3, concat_axis=2, tiled=True)
    source = jnp.arange(count, dtype=jnp.int32)
    target = jnp.arange(2 * count, dtype=jnp.int32)
    angle = math.pi / count * (source[:, None] * target[None, :] % (2 * count)).astype(jnp.float32)
    table = jnp.stack([jnp.cos(angle), -jnp.sin(angle)])
    summed = jnp.einsum("xak,xrkb->rab", table, spread, precision=highest)
    result = lax.all_to_all(summed, "seq", split_axis=1, concat_axis=2, tiled=True)[:, 0, :]
    return result * (1.0 / total)


def local(inputs, proj_weight, short_taps, skip_gain, filters, out_weight):
    channels = inputs.shape[0]
    length = inputs.shape[1]
    columns = proj_weight
    summed = lax.psum_scatter(
        jnp.einsum("sio,it->ost", columns, inputs, preferred_element_type=jnp.float32),
        "ch",
        scatter_dimension=0,
        tiled=True,
    )
    projected = summed.astype(jnp.bfloat16)
    before = passed_along(projected[:, :, length - 2 :], "seq", 1)
    padded = jnp.concatenate([before, projected], axis=2).astype(jnp.float32)
    conv_in = (
        short_taps[:, :, 0:1] * padded[:, :, 2:]
        + short_taps[:, :, 1:2] * padded[:, :, 1:-1]
        + short_taps[:, :, 2:3] * padded[:, :, :-2]
    )
    values = conv_in[:, 0, :]
    first_gate = conv_in[:, 1, :]
    second_gate = conv_in[:, 2, :]
    spectra = forward(jnp.concatenate([values, filters[0], filters[1]], axis=0))
    value_spectrum = spectra[:, :channels]
    first_filter = spectra[:, channels : 2 * channels]
    second_filter = spectra[:, 2 * channels :]
    first = inverse(complex_product(value_spectrum, first_filter)) + skip_gain[:, 0:1] * values
    gated = first_gate * first
    second = inverse(complex_product(forward(gated), second_filter)) + skip_gain[:, 1:2] * gated
    mixed = (second_gate * second).astype(jnp.bfloat16)
    columns = out_weight
    result = lax.psum_scatter(
        jnp.einsum("io,it->ot", columns, mixed, preferred_element_type=jnp.float32),
        "ch",
        scatter_dimension=0,
        tiled=True,
    )
    return result.astype(jnp.bfloat16)


MESH = pl.DeviceIdType.MESH
LANES = 128


def kernel(
    S,
    C,
    in_ref,
    pw_ref,
    taps_ref,
    skip_ref,
    f_ref,
    ow_ref,
    out_ref,
    in_buf,
    pw_buf,
    ow_buf,
    send_f,
    recv_f,
    send_p,
    recv_p,
    send_m,
    recv_m,
    hs,
    ps,
    ms,
    xp,
    toep,
    y_send,
    y_recv,
    f_send,
    f_recv,
    p_send,
    p_recv,
    m_send,
    m_recv,
):
    s = lax.axis_index("seq")
    c = lax.axis_index("ch")
    N = S * C
    me = s * C + c
    CL, L = in_ref.shape
    K = CL // S
    nb = L // LANES
    NB = S * nb

    barrier = pltpu.get_barrier_semaphore()

    def greet(i, carry):
        peer = lax.rem(me + i, N)
        pl.semaphore_signal(
            barrier, inc=1, device_id=(peer // C, lax.rem(peer, C)), device_id_type=MESH
        )
        return carry

    lax.fori_loop(1, N, greet, 0)

    def pack(d, carry):
        rows = pl.ds(pl.multiple_of(d * K, K), K)
        parts = []
        for j in range(nb):
            for f in range(2):
                parts.append(f_ref[f, rows, j * LANES : (j + 1) * LANES])
        send_f[d] = jnp.concatenate(parts, axis=0).astype(jnp.bfloat16)
        return carry

    lax.fori_loop(0, S, pack, 0)
    recv_f[s] = send_f[s]
    own = pl.ds(pl.multiple_of(c * CL, CL), CL)
    in_buf[c] = in_ref[...]
    pw_buf[c] = pw_ref[:, :, own]
    ow_buf[c] = ow_ref[:, own]

    pl.semaphore_wait(barrier, N - 1)

    def swap(i, n, to, slot):
        cut = pl.ds(pl.multiple_of(to * CL, CL), CL)
        source, target = [
            (in_ref, in_buf),
            (pw_ref.at[:, :, cut], pw_buf),
            (ow_ref.at[:, cut], ow_buf),
        ][n]
        return pltpu.make_async_remote_copy(
            src_ref=source,
            dst_ref=target.at[slot],
            send_sem=y_send.at[n, i],
            recv_sem=y_recv.at[n, slot],
            device_id=(s, to),
            device_id_type=MESH,
        )

    for i in range(1, C):
        for n in range(3):
            swap(i, n, lax.rem(c + i, C), c).start()

    def filter_copy(i, to, slot):
        return pltpu.make_async_remote_copy(
            src_ref=send_f.at[to],
            dst_ref=recv_f.at[slot],
            send_sem=f_send.at[i],
            recv_sem=f_recv.at[slot],
            device_id=(to, c),
            device_id_type=MESH,
        )

    def start_filter(i, carry):
        filter_copy(i, lax.rem(s + i, S), s).start()
        return carry

    lax.fori_loop(1, S, start_filter, 0)

    def wait_swap(n):
        for i in range(1, C):
            swap(i, n, lax.rem(c + i, C), lax.rem(c + C - i, C)).wait_recv()

    def group_copy(g, i, to, slot):
        return pltpu.make_async_remote_copy(
            src_ref=send_p.at[g, to],
            dst_ref=recv_p.at[g, slot],
            send_sem=p_send.at[g, i],
            recv_sem=p_recv.at[g, slot],
            device_id=(to, c),
            device_id_type=MESH,
        )

    wait_swap(0)
    wait_swap(1)
    signal = in_buf[...].reshape(C * CL, L)
    for g in range(3):
        weight = pw_buf[:, g].reshape(C * CL, CL)
        part = lax.dot_general(
            weight, signal, (((0,), (0,)), ((), ())), preferred_element_type=jnp.float32
        )
        for d in range(S):
            send_p[g, d] = jnp.concatenate(
                [
                    part[d * K : (d + 1) * K, j * LANES : (j + 1) * LANES]
                    for j in range(nb)
                ],
                axis=0,
            ).astype(jnp.bfloat16)
        recv_p[g, s] = send_p[g, s]

        def start_group(i, carry):
            group_copy(g, i, lax.rem(s + i, S), s).start()
            return carry

        lax.fori_loop(1, S, start_group, 0)

    def wait_filter(i, carry):
        filter_copy(i, lax.rem(s + i, S), lax.rem(s + S - i, S)).wait_recv()
        return carry

    lax.fori_loop(1, S, wait_filter, 0)
    hs[...] = recv_f[...].reshape(NB * 2 * K, LANES).astype(jnp.float32)
    xp[...] = jnp.zeros_like(xp)
    lane = lax.broadcasted_iota(jnp.int32, (LANES, LANES), 1)
    below = lax.broadcasted_iota(jnp.int32, (LANES, LANES), 0)
    upper = lane >= below

    def build(q, carry):
        def block(m, previous):
            row = hs[pl.ds(m * (2 * K) + q, 1), :]
            turned = pltpu.roll(
                jnp.broadcast_to(row, (LANES, LANES)), 0, 1, stride=1, stride_axis=0
            )
            toep[q, pl.ds(pl.multiple_of(m * LANES, LANES), LANES), :] = jnp.where(
                upper, turned, previous
            ).astype(jnp.bfloat16)
            return turned

        lax.fori_loop(0, NB, block, jnp.zeros((LANES, LANES), jnp.float32), unroll=4)
        return carry

    lax.fori_loop(0, 2 * K, build, 0)

    for g in range(3):

        def wait_group(i, carry):
            group_copy(g, i, lax.rem(s + i, S), lax.rem(s + S - i, S)).wait_recv()
            return carry

        lax.fori_loop(1, S, wait_group, 0)
        ps[g] = recv_p[g].reshape(NB * K, LANES).astype(jnp.float32)

    column = lax.broadcasted_iota(jnp.int32, (NB, LANES), 1)
    token_block = lax.broadcasted_iota(jnp.int32, (NB, LANES), 0)

    def delayed(x, by):
        turned = pltpu.roll(x, by, 1)
        carried = jnp.where(token_block == 0, 0.0, pltpu.roll(turned, 1, 0))
        return jnp.where(column < by, carried, turned)

    def long_filter(x, q):
        xp[NB : 2 * NB, 0:LANES] = x
        xp[NB + 1 : 2 * NB + 1, LANES : 2 * LANES] = x
        half = NB // 2
        low = jnp.zeros((NB, LANES), jnp.float32)
        high = jnp.zeros((half, LANES), jnp.float32)
        for p in range(NB // 2):
            block = toep[q, 2 * LANES * p : 2 * LANES * (p + 1), :]
            if 2 * p < half:
                rows = xp[NB - 2 * p : 2 * NB - 2 * p, :].astype(jnp.bfloat16)
                low += jnp.dot(rows, block, preferred_element_type=jnp.float32)
            else:
                rows = xp[NB + half - 2 * p : 2 * NB - 2 * p, :].astype(jnp.bfloat16)
                high += jnp.dot(rows, block, preferred_element_type=jnp.float32)
        return jnp.concatenate([low[:half], low[half:] + high], axis=0)

    def channel(k, carry):
        row = s * K + k
        taps = taps_ref[row]
        gains = skip_ref[pl.ds(row, 1), :]
        conv = []
        for g in range(3):
            x = ps[g, pl.ds(k, NB, stride=K), :]
            conv.append(
                taps[g : g + 1, 0:1] * x
                + taps[g : g + 1, 1:2] * delayed(x, 1)
                + taps[g : g + 1, 2:3] * delayed(x, 2)
            )
        first = long_filter(conv[0], k) + gains[:, 0:1] * conv[0]
        gated = conv[1] * first
        second = long_filter(gated, K + k) + gains[:, 1:2] * gated
        ms[pl.ds(k, NB, stride=K), :] = conv[2] * second
        return carry

    lax.fori_loop(0, K, channel, 0)

    def mixed_copy(i, slot):
        peer = lax.rem(me + i, N)
        to = peer // C
        return pltpu.make_async_remote_copy(
            src_ref=send_m.at[to],
            dst_ref=recv_m.at[slot],
            send_sem=m_send.at[i],
            recv_sem=m_recv.at[slot],
            device_id=(to, lax.rem(peer, C)),
            device_id_type=MESH,
        )

    send_m[...] = ms[...].reshape(S, nb * K, LANES).astype(jnp.bfloat16)

    def start_mixed(i, carry):
        mixed_copy(i, c * S + s).start()
        return carry

    lax.fori_loop(1, N, start_mixed, 0)
    recv_m[c * S + s] = send_m[s]
    wait_swap(2)
    weight = ow_buf[...].reshape(C * CL, CL)

    def wait_mixed(i, carry):
        peer = lax.rem(me + N - i, N)
        mixed_copy(i, lax.rem(peer, C) * S + peer // C).wait_recv()
        return carry

    lax.fori_loop(1, N, wait_mixed, 0)
    mixed = recv_m[...].astype(jnp.float32)
    mixed = jnp.concatenate(
        [mixed[:, j * K : (j + 1) * K, :].reshape(N * K, LANES) for j in range(nb)],
        axis=1,
    ).astype(jnp.bfloat16)
    out_ref[...] = lax.dot_general(
        weight, mixed, (((0,), (0,)), ((), ())), preferred_element_type=jnp.float32
    ).astype(out_ref.dtype)

    for i in range(1, C):
        for n in range(3):
            swap(i, n, lax.rem(c + i, C), c).wait_send()

    def drain(i, carry):
        filter_copy(i, lax.rem(s + i, S), s).wait_send()
        for g in range(3):
            group_copy(g, i, lax.rem(s + i, S), s).wait_send()
        return carry

    lax.fori_loop(1, S, drain, 0)

    def drain_mixed(i, carry):
        mixed_copy(i, c * S + s).wait_send()
        return carry

    lax.fori_loop(1, N, drain_mixed, 0)


def fused(S, C, inputs, proj_weight, short_taps, skip_gain, filters, out_weight):
    CL, L = inputs.shape
    K = CL // S
    nb = L // LANES
    NB = S * nb
    N = S * C
    half, full = jnp.bfloat16, jnp.float32
    dma = pltpu.SemaphoreType.DMA
    vmem = pl.BlockSpec(memory_space=pltpu.VMEM)
    return pl.pallas_call(
        functools.partial(kernel, S, C),
        out_shape=jax.ShapeDtypeStruct((CL, L), half),
        in_specs=[vmem] * 6,
        out_specs=vmem,
        scratch_shapes=[
            pltpu.VMEM((C, CL, L), half),
            pltpu.VMEM((C, 3, CL, CL), half),
            pltpu.VMEM((C, CL, CL), half),
            pltpu.VMEM((S, nb * 2 * K, LANES), half),
            pltpu.VMEM((S, nb * 2 * K, LANES), half),
            pltpu.VMEM((3, S, nb * K, LANES), half),
            pltpu.VMEM((3, S, nb * K, LANES), half),
            pltpu.VMEM((S, nb * K, LANES), half),
            pltpu.VMEM((N, nb * K, LANES), half),
            pltpu.VMEM((NB * 2 * K, LANES), full),
            pltpu.VMEM((3, NB * K, LANES), full),
            pltpu.VMEM((NB * K, LANES), full),
            pltpu.VMEM((2 * NB + 8, 2 * LANES), full),
            pltpu.VMEM((2 * K, NB * LANES, LANES), half),
            dma((3, C)),
            dma((3, C)),
            dma((S,)),
            dma((S,)),
            dma((3, S)),
            dma((3, S)),
            dma((N,)),
            dma((N,)),
        ],
        compiler_params=pltpu.CompilerParams(
            collective_id=0, has_side_effects=True, vmem_limit_bytes=VMEM_LIMIT
        ),
    )(inputs, proj_weight, short_taps, skip_gain, filters, out_weight)


VMEM_LIMIT = 56 * 1024 * 1024


def fits(S, C, CL, L):
    K = CL // S
    toeplitz = 2 * K * S * L * LANES * 2
    return (
        C > 1
        and S > 1
        and CL % (8 * S) == 0
        and CL % LANES == 0
        and L % LANES == 0
        and (S * L // LANES) % 16 == 0
        and toeplitz <= 40 * 1024 * 1024
    )


def solution(mesh):
    in_specs = (
        P("ch", "seq"),
        P(None, "ch", None),
        P("ch", None, None),
        P("ch", None),
        P(None, "ch", "seq"),
        P("ch", None),
    )
    out_specs = P("ch", "seq")
    S, C = mesh.shape["seq"], mesh.shape["ch"]

    def body(*shards):
        if fits(S, C, *shards[0].shape):
            return fused(S, C, *shards)
        return local(*shards)

    return jax.shard_map(body, mesh=mesh, in_specs=in_specs, out_specs=out_specs, check_vma=False)
```

profile of v0, /device:TPU:0, one launch (start us, length us, event | category | flops | bytes accessed | tf_op | source)
XLA Modules:
  0.0 68.4 jit_solution(5359654906096768661)
XLA Ops:
  0.0 0.0 copy-start
  0.0 1.4 %copy.8.skip_ref = f32[128,2]{1,0:T(8,128)} copy(f32[128,2]{0,1:T(2,128)} %param.9) | data formatting | bytes 2048 | tf_op args[3]
  1.4 0.0 copy-done
  1.4 0.8 %copy.7.taps_ref = f32[128,3,3]{2,1,0:T(4,128)} copy(f32[128,3,3]{0,2,1:T(4,128)S(1)} %copy-done) | data formatting | bytes 9216 | tf_op args[2]
  2.3 64.5 %shard_map.64 = bf16[128,512]{1,0:T(8,128)(2,1)} custom-call(bf16[128,512]{1,0:T(8,128)(2,1)} %in_ref.1, bf16[3,128,256]{2,1,0:T(8,128)(2,1)} %pw_ref.1, f32[128,3,3]{2,1,0:T(4,128)} %copy.7.taps_ref, f32[128,2]{1,0:T(8,128)} %copy.8.skip_ref, f32[2,128,512]{2,1,0:T(8,128)} %f_ref.1, bf16[128,256]{1,0:T(8,128)(2,1)} %ow_ref.1), custom_call_target="tpu_custom_call" | custom-call | tf_op jit(solution)/shard_map/pallas_call | solution.py:437
  66.8 1.6 %copy.10 = bf16[128,512]{1,0:T(8,128)(2,1)} copy(bf16[128,512]{1,0:T(8,128)(2,1)} %shard_map.64) | data formatting | bytes 262144
Async XLA Ops:
  0.0 1.4 %copy-start = (f32[128,3,3]{0,2,1:T(4,128)S(1)}, f32[128,3,3]{0,2,1:T(4,128)}, u32[]{:S(2)}) copy-start(f32[128,3,3]{0,2,1:T(4,128)} %param.8) | copy-start | bytes 13828
where the time goes:
time: 68.6 us; the launch traced here: 68.4 us
  Pallas kernels  64.5 us (94%)
  local copies, waits for them, and re-layouts  3.85 us (6%)
    pallas_call x1, Pallas kernels, fused(): pl.pallas_call(functools.partial(kernel, S, C), out_shape=jax.ShapeDtypeS...  64.5 us
    unnamed x5, local copies, waits for them, and re-layouts  3.85 us

commit v1 on v0

--- a/solution.py
+++ b/solution.py
@@ -295,22 +295,43 @@
     lax.fori_loop(1, S, wait_filter, 0)
     hs[...] = recv_f[...].reshape(NB * 2 * K, LANES).astype(jnp.float32)
     xp[...] = jnp.zeros_like(xp)
-    lane = lax.broadcasted_iota(jnp.int32, (LANES, LANES), 1)
-    below = lax.broadcasted_iota(jnp.int32, (LANES, LANES), 0)
-    upper = lane >= below
+    lane = lax.broadcasted_iota(jnp.int32, (16, LANES), 1)
+    below = lax.broadcasted_iota(jnp.int32, (16, LANES), 0)
+    half = NB // 2
 
     def build(q, carry):
-        def block(m, previous):
+        def block(m, previous, side):
             row = hs[pl.ds(m * (2 * K) + q, 1), :]
             turned = pltpu.roll(
-                jnp.broadcast_to(row, (LANES, LANES)), 0, 1, stride=1, stride_axis=0
+                jnp.broadcast_to(row, (16, LANES)), 0, 1, stride=1, stride_axis=0
             )
-            toep[q, pl.ds(pl.multiple_of(m * LANES, LANES), LANES), :] = jnp.where(
-                upper, turned, previous
-            ).astype(jnp.bfloat16)
-            return turned
-
-        lax.fori_loop(0, NB, block, jnp.zeros((LANES, LANES), jnp.float32), unroll=4)
+            base = jnp.where(lane >= below, turned, previous[0]).astype(jnp.bfloat16)
+            kept = [turned]
+            parts = []
+            for g in range(LANES // 16):
+                moved = base if g == 0 else pltpu.roll(base, 16 * g, 1)
+                if g == 0:
+                    parts.append(base)
+                else:
+                    parts.append(jnp.where(lane >= 16 * g, moved, previous[g]))
+                    kept.append(moved)
+            place = pl.multiple_of((m - side * half) * LANES, LANES)
+            toep[q, pl.ds(place, LANES), side * LANES : (side + 1) * LANES] = (
+                jnp.concatenate(parts, axis=0)
+            )
+            return tuple(kept)
+
+        state = (jnp.zeros((16, LANES), jnp.float32),) + tuple(
+            jnp.zeros((16, LANES), jnp.bfloat16) for g in range(1, LANES // 16)
+        )
+        for side in range(2):
+            state = lax.fori_loop(
+                side * half,
+                (side + 1) * half,
+                functools.partial(block, side=side),
+                state,
+                unroll=4,
+            )
         return carry
 
     lax.fori_loop(0, 2 * K, build, 0)
@@ -332,41 +353,51 @@
         carried = jnp.where(token_block == 0, 0.0, pltpu.roll(turned, 1, 0))
         return jnp.where(column < by, carried, turned)
 
-    def long_filter(x, q):
-        xp[NB : 2 * NB, 0:LANES] = x
-        xp[NB + 1 : 2 * NB + 1, LANES : 2 * LANES] = x
-        half = NB // 2
-        low = jnp.zeros((NB, LANES), jnp.float32)
-        high = jnp.zeros((half, LANES), jnp.float32)
-        for p in range(NB // 2):
-            block = toep[q, 2 * LANES * p : 2 * LANES * (p + 1), :]
-            if 2 * p < half:
-                rows = xp[NB - 2 * p : 2 * NB - 2 * p, :].astype(jnp.bfloat16)
-                low += jnp.dot(rows, block, preferred_element_type=jnp.float32)
-            else:
-                rows = xp[NB + half - 2 * p : 2 * NB - 2 * p, :].astype(jnp.bfloat16)
-                high += jnp.dot(rows, block, preferred_element_type=jnp.float32)
-        return jnp.concatenate([low[:half], low[half:] + high], axis=0)
-
-    def channel(k, carry):
-        row = s * K + k
-        taps = taps_ref[row]
-        gains = skip_ref[pl.ds(row, 1), :]
-        conv = []
-        for g in range(3):
-            x = ps[g, pl.ds(k, NB, stride=K), :]
-            conv.append(
-                taps[g : g + 1, 0:1] * x
-                + taps[g : g + 1, 1:2] * delayed(x, 1)
-                + taps[g : g + 1, 2:3] * delayed(x, 2)
+    def long_filter(x, q, at):
+        xp[at, NB : 2 * NB, 0:LANES] = x
+        xp[at, NB + 1 : 2 * NB + 1, LANES : 2 * LANES] = x
+        rows = jnp.concatenate(
+            [
+                xp[at, NB - 2 * p : 2 * NB - 2 * p, :].astype(jnp.bfloat16)
+                for p in range(half // 2)
+            ],
+            axis=1,
+        )
+        both = jnp.dot(rows, toep[q], preferred_element_type=jnp.float32)
+        near, far = both[:, :LANES], both[:half, LANES:]
+        return jnp.concatenate([near[:half], near[half:] + far], axis=0)
+
+    def channels(pair, carry):
+        ks = [2 * pair, 2 * pair + 1]
+        conv, gains = [], []
+        for k in ks:
+            mine = lanes == s * K + k
+            taps = jnp.sum(jnp.where(mine, taps_ref[...], 0.0), axis=2, keepdims=True)
+            gains.append(
+                jnp.sum(jnp.where(mine[0], skip_ref[...], 0.0), axis=1, keepdims=True)
             )
-        first = long_filter(conv[0], k) + gains[:, 0:1] * conv[0]
-        gated = conv[1] * first
-        second = long_filter(gated, K + k) + gains[:, 1:2] * gated
-        ms[pl.ds(k, NB, stride=K), :] = conv[2] * second
-        return carry
-
-    lax.fori_loop(0, K, channel, 0)
+            parts = []
+            for g in range(3):
+                x = ps[g, pl.ds(k, NB, stride=K), :]
+                parts.append(
+                    taps[g, 0:1] * x
+                    + taps[g, 1:2] * delayed(x, 1)
+                    + taps[g, 2:3] * delayed(x, 2)
+                )
+            conv.append(parts)
+        gated = [
+            conv[n][1]
+            * (long_filter(conv[n][0], ks[n], 2 * n) + gains[n][0:1] * conv[n][0])
+            for n in range(2)
+        ]
+        for n in range(2):
+            second = long_filter(gated[n], K + ks[n], 2 * n + 1)
+            second = second + gains[n][1:2] * gated[n]
+            ms[pl.ds(ks[n], NB, stride=K), :] = conv[n][2] * second
+        return carry
+
+    lanes = lax.broadcasted_iota(jnp.int32, (1, 1, taps_ref.shape[2]), 2)
+    lax.fori_loop(0, K // 2, channels, 0)
 
     def mixed_copy(i, slot):
         peer = lax.rem(me + i, N)
@@ -452,8 +483,8 @@
             pltpu.VMEM((NB * 2 * K, LANES), full),
             pltpu.VMEM((3, NB * K, LANES), full),
             pltpu.VMEM((NB * K, LANES), full),
-            pltpu.VMEM((2 * NB + 8, 2 * LANES), full),
-            pltpu.VMEM((2 * K, NB * LANES, LANES), half),
+            pltpu.VMEM((4, 2 * NB + 8, 2 * LANES), full),
+            pltpu.VMEM((2 * K, NB // 2 * LANES, 2 * LANES), half),
             dma((3, C)),
             dma((3, C)),
             dma((S,)),
@@ -466,7 +497,14 @@
         compiler_params=pltpu.CompilerParams(
             collective_id=0, has_side_effects=True, vmem_limit_bytes=VMEM_LIMIT
         ),
-    )(inputs, proj_weight, short_taps, skip_gain, filters, out_weight)
+    )(
+        inputs,
+        proj_weight,
+        short_taps.transpose(1, 2, 0),
+        skip_gain.T,
+        filters,
+        out_weight,
+    )
 
 
 VMEM_LIMIT = 56 * 1024 * 1024

time: 68.6 us -> 78.6 us (1.15)
  Pallas kernels: 64.5 us -> 76.9 us
  local copies, waits for them, and re-layouts: 3.85 us -> 1.57 us
    pallas_call x1, Pallas kernels: 64.5 us -> 76.9 us  [fused(): pl.pallas_call(functools.partial(kernel, S, C), out_shape=jax.ShapeDtypeS...]
    unnamed x5 -> x1, local copies, waits for them, and re-layouts: 3.85 us -> 1.57 us
where the time goes in v1:
time: 78.6 us; the launch traced here: 78.5 us
  Pallas kernels  76.9 us (98%)
  local copies, waits for them, and re-layouts  1.57 us (2%)
    pallas_call x1, Pallas kernels, fused(): pl.pallas_call(functools.partial(kernel, S, C), out_shape=jax.ShapeDtypeS...  76.9 us

profile of v1, /device:TPU:0, one launch (start us, length us, event | category | flops | bytes accessed | tf_op | source)
XLA Modules:
  0.0 78.5 jit_solution(9949016998754923425)
XLA Ops:
  0.0 76.9 %shard_map.64 = bf16[128,512]{1,0:T(8,128)(2,1)} custom-call(bf16[128,512]{1,0:T(8,128)(2,1)} %in_ref.1, bf16[3,128,256]{2,1,0:T(8,128)(2,1)} %pw_ref.1, f32[3,3,128]{2,1,0:T(4,128)} %bitcast.2, f32[2,128]{1,0:T(2,128)} %bitcast.3, f32[2,128,512]{2,1,0:T(8,128)} %f_ref.1, bf16[128,256]{1,0:T(8,128)(2,1)} %ow_ref.1), custom_call_target="tpu_custom_call" | custom-call | tf_op jit(solution)/shard_map/pallas_call | solution.py:468
  76.9 1.6 %copy.8 = bf16[128,512]{1,0:T(8,128)(2,1)} copy(bf16[128,512]{1,0:T(8,128)(2,1)} %shard_map.64) | data formatting | bytes 262144

commit v2 on v1

--- a/solution.py
+++ b/solution.py
@@ -141,6 +141,8 @@
 
 MESH = pl.DeviceIdType.MESH
 LANES = 128
+SEG = 32
+PARTS = 8
 
 
 def kernel(
@@ -167,6 +169,8 @@
     ms,
     xp,
     toep,
+    heads,
+    tails,
     y_send,
     y_recv,
     f_send,
@@ -295,43 +299,45 @@
     lax.fori_loop(1, S, wait_filter, 0)
     hs[...] = recv_f[...].reshape(NB * 2 * K, LANES).astype(jnp.float32)
     xp[...] = jnp.zeros_like(xp)
-    lane = lax.broadcasted_iota(jnp.int32, (16, LANES), 1)
-    below = lax.broadcasted_iota(jnp.int32, (16, LANES), 0)
-    half = NB // 2
+    U = NB // PARTS
+    V = LANES // SEG
+    count = U * V
+    lane = lax.broadcasted_iota(jnp.int32, (8, LANES), 1)
+    below = lax.broadcasted_iota(jnp.int32, (8, LANES), 0)
+    wide_lane = lax.broadcasted_iota(jnp.int32, (U, LANES), 1)
 
     def build(q, carry):
-        def block(m, previous, side):
-            row = hs[pl.ds(m * (2 * K) + q, 1), :]
-            turned = pltpu.roll(
-                jnp.broadcast_to(row, (16, LANES)), 0, 1, stride=1, stride_axis=0
+        h = hs[pl.ds(q, NB, stride=2 * K), :]
+        last = jnp.zeros((1, LANES), jnp.float32)
+        for w in range(PARTS // V):
+            for v in range(V):
+                here = None
+                for n in range(V):
+                    rows = h[U * (V * w + n) : U * (V * w + n + 1)]
+                    by = SEG * (n - v) % LANES
+                    moved = pltpu.roll(rows, by, 1) if by else rows
+                    here = moved if n == 0 else jnp.where(wide_lane >= SEG * n, moved, here)
+                heads[w, pl.ds(v, U, stride=V), :] = here
+                tails[w, pl.ds(v + 1, U, stride=V), :] = pltpu.roll(here, LANES - SEG, 1)
+            tails[w, 0:1, :] = jnp.where(
+                wide_lane[0:1] < LANES - SEG, here[U - 1 : U], last
             )
-            base = jnp.where(lane >= below, turned, previous[0]).astype(jnp.bfloat16)
-            kept = [turned]
-            parts = []
-            for g in range(LANES // 16):
-                moved = base if g == 0 else pltpu.roll(base, 16 * g, 1)
-                if g == 0:
-                    parts.append(base)
-                else:
-                    parts.append(jnp.where(lane >= 16 * g, moved, previous[g]))
-                    kept.append(moved)
-            place = pl.multiple_of((m - side * half) * LANES, LANES)
-            toep[q, pl.ds(place, LANES), side * LANES : (side + 1) * LANES] = (
-                jnp.concatenate(parts, axis=0)
-            )
-            return tuple(kept)
-
-        state = (jnp.zeros((16, LANES), jnp.float32),) + tuple(
-            jnp.zeros((16, LANES), jnp.bfloat16) for g in range(1, LANES // 16)
-        )
-        for side in range(2):
-            state = lax.fori_loop(
-                side * half,
-                (side + 1) * half,
-                functools.partial(block, side=side),
-                state,
-                unroll=4,
-            )
+            last = here[U - 1 : U]
+
+        @pl.loop(0, count, unroll=4)
+        def _(m):
+            place = pl.multiple_of((count - 1 - m) * SEG, SEG)
+            for w in range(PARTS // V):
+                head = jnp.broadcast_to(heads[w, pl.ds(m, 1), :], (8, LANES))
+                tail = jnp.broadcast_to(tails[w, pl.ds(m, 1), :], (8, LANES))
+                parts = []
+                for g in range(SEG // 8):
+                    source = jnp.where(lane % SEG + below < SEG - 8 * g, head, tail)
+                    parts.append(pltpu.roll(source, 8 * g, 1, stride=1, stride_axis=0))
+                toep[q, pl.ds(place, SEG), w * LANES : (w + 1) * LANES] = (
+                    jnp.concatenate(parts, axis=0).astype(jnp.bfloat16)
+                )
+
         return carry
 
     lax.fori_loop(0, 2 * K, build, 0)
@@ -353,19 +359,49 @@
         carried = jnp.where(token_block == 0, 0.0, pltpu.roll(turned, 1, 0))
         return jnp.where(column < by, carried, turned)
 
+    def down(x, by):
+        if by == 0:
+            return x
+        return jnp.concatenate(
+            [jnp.zeros((by, LANES), jnp.float32), x[: NB - by]], axis=0
+        )
+
+    segment = column // SEG
+
     def long_filter(x, q, at):
-        xp[at, NB : 2 * NB, 0:LANES] = x
-        xp[at, NB + 1 : 2 * NB + 1, LANES : 2 * LANES] = x
+        for r in range(V):
+            by = LANES - SEG * (r + 1)
+            xp[at, r, U : U + NB, :] = delayed(x, by) if by else x
         rows = jnp.concatenate(
             [
-                xp[at, NB - 2 * p : 2 * NB - 2 * p, :].astype(jnp.bfloat16)
-                for p in range(half // 2)
+                jnp.concatenate(
+                    [
+                        xp[at, r, t + 1 : t + 1 + NB, :].astype(jnp.bfloat16)
+                        for t in range(U)
+                    ],
+                    axis=1,
+                )
+                for r in range(V)
             ],
-            axis=1,
+            axis=0,
         )
         both = jnp.dot(rows, toep[q], preferred_element_type=jnp.float32)
-        near, far = both[:, :LANES], both[:half, LANES:]
-        return jnp.concatenate([near[:half], near[half:] + far], axis=0)
+        total = None
+        for d in range(V):
+            part = None
+            for n in range(V):
+                r = (n + d) % V
+                piece = sum(
+                    down(
+                        both[r * NB : (r + 1) * NB, w * LANES : (w + 1) * LANES],
+                        U * (V * w + n),
+                    )
+                    for w in range(PARTS // V)
+                )
+                part = piece if n == 0 else jnp.where(segment >= n, piece, part)
+            part = pltpu.roll(part, SEG * d, 1) if d else part
+            total = part if d == 0 else total + part
+        return total
 
     def channels(pair, carry):
         ks = [2 * pair, 2 * pair + 1]
@@ -483,8 +519,12 @@
             pltpu.VMEM((NB * 2 * K, LANES), full),
             pltpu.VMEM((3, NB * K, LANES), full),
             pltpu.VMEM((NB * K, LANES), full),
-            pltpu.VMEM((4, 2 * NB + 8, 2 * LANES), full),
-            pltpu.VMEM((2 * K, NB // 2 * LANES, 2 * LANES), half),
+            pltpu.VMEM((4, LANES // SEG, NB + NB // PARTS, LANES), full),
+            pltpu.VMEM((2 * K, NB // PARTS * LANES, PARTS * SEG), half),
+            pltpu.VMEM((PARTS * SEG // LANES, NB // PARTS * (LANES // SEG), LANES), full),
+            pltpu.VMEM(
+                (PARTS * SEG // LANES, (NB // PARTS + 2) * (LANES // SEG), LANES), full
+            ),
             dma((3, C)),
             dma((3, C)),
             dma((S,)),
@@ -512,14 +552,14 @@
 
 def fits(S, C, CL, L):
     K = CL // S
-    toeplitz = 2 * K * S * L * LANES * 2
+    toeplitz = 2 * K * S * L * SEG * 2
     return (
         C > 1
         and S > 1
         and CL % (8 * S) == 0
         and CL % LANES == 0
         and L % LANES == 0
-        and (S * L // LANES) % 16 == 0
+        and (S * L // LANES) % (8 * PARTS) == 0
         and toeplitz <= 40 * 1024 * 1024
     )
 

time: 78.6 us -> 47.2 us (0.60)
  Pallas kernels: 76.9 us -> 45.5 us
    pallas_call x1, Pallas kernels: 76.9 us -> 45.5 us  [fused(): pl.pallas_call(functools.partial(kernel, S, C), out_shape=jax.ShapeDtypeS...]
where the time goes in v2:
time: 47.2 us; the launch traced here: 47.1 us
  Pallas kernels  45.5 us (96%)
  local copies, waits for them, and re-layouts  1.57 us (3%)
    pallas_call x1, Pallas kernels, fused(): pl.pallas_call(functools.partial(kernel, S, C), out_shape=jax.ShapeDtypeS...  45.5 us
    unnamed x1, local copies, waits for them, and re-layouts  1.57 us

profile of v2, /device:TPU:0, one launch (start us, length us, event | category | flops | bytes accessed | tf_op | source)
XLA Modules:
  0.0 47.1 jit_solution(7522605195267529949)
XLA Ops:
  0.0 45.5 %shard_map.64 = bf16[128,512]{1,0:T(8,128)(2,1)} custom-call(bf16[128,512]{1,0:T(8,128)(2,1)} %in_ref.1, bf16[3,128,256]{2,1,0:T(8,128)(2,1)} %pw_ref.1, f32[3,3,128]{2,1,0:T(4,128)} %bitcast.2, f32[2,128]{1,0:T(2,128)} %bitcast.3, f32[2,128,512]{2,1,0:T(8,128)} %f_ref.1, bf16[128,256]{1,0:T(8,128)(2,1)} %ow_ref.1), custom_call_target="tpu_custom_call" | custom-call | tf_op jit(solution)/shard_map/pallas_call | solution.py:504
  45.5 1.6 %copy.8 = bf16[128,512]{1,0:T(8,128)(2,1)} copy(bf16[128,512]{1,0:T(8,128)(2,1)} %shard_map.64) | data formatting | bytes 262144

commit v3 on v2

--- a/solution.py
+++ b/solution.py
@@ -221,13 +221,15 @@
     def swap(i, n, to, slot):
         cut = pl.ds(pl.multiple_of(to * CL, CL), CL)
         source, target = [
-            (in_ref, in_buf),
-            (pw_ref.at[:, :, cut], pw_buf),
-            (ow_ref.at[:, cut], ow_buf),
+            (in_ref, in_buf.at[slot]),
+            (pw_ref.at[0, :, cut], pw_buf.at[slot, 0]),
+            (pw_ref.at[1, :, cut], pw_buf.at[slot, 1]),
+            (pw_ref.at[2, :, cut], pw_buf.at[slot, 2]),
+            (ow_ref.at[:, cut], ow_buf.at[slot]),
         ][n]
         return pltpu.make_async_remote_copy(
             src_ref=source,
-            dst_ref=target.at[slot],
+            dst_ref=target,
             send_sem=y_send.at[n, i],
             recv_sem=y_recv.at[n, slot],
             device_id=(s, to),
@@ -235,7 +237,7 @@
         )
 
     for i in range(1, C):
-        for n in range(3):
+        for n in range(5):
             swap(i, n, lax.rem(c + i, C), c).start()
 
     def filter_copy(i, to, slot):
@@ -269,9 +271,9 @@
         )
 
     wait_swap(0)
-    wait_swap(1)
     signal = in_buf[...].reshape(C * CL, L)
     for g in range(3):
+        wait_swap(1 + g)
         weight = pw_buf[:, g].reshape(C * CL, CL)
         part = lax.dot_general(
             weight, signal, (((0,), (0,)), ((), ())), preferred_element_type=jnp.float32
@@ -455,7 +457,7 @@
 
     lax.fori_loop(1, N, start_mixed, 0)
     recv_m[c * S + s] = send_m[s]
-    wait_swap(2)
+    wait_swap(4)
     weight = ow_buf[...].reshape(C * CL, CL)
 
     def wait_mixed(i, carry):
@@ -474,7 +476,7 @@
     ).astype(out_ref.dtype)
 
     for i in range(1, C):
-        for n in range(3):
+        for n in range(5):
             swap(i, n, lax.rem(c + i, C), c).wait_send()
 
     def drain(i, carry):
@@ -525,8 +527,8 @@
             pltpu.VMEM(
                 (PARTS * SEG // LANES, (NB // PARTS + 2) * (LANES // SEG), LANES), full
             ),
-            dma((3, C)),
-            dma((3, C)),
+            dma((5, C)),
+            dma((5, C)),
             dma((S,)),
             dma((S,)),
             dma((3, S)),

time: 47.2 us -> 46.4 us (0.983)
  Pallas kernels: 45.5 us -> 44.7 us
    pallas_call x1, Pallas kernels: 45.5 us -> 44.7 us  [fused(): pl.pallas_call(functools.partial(kernel, S, C), out_shape=jax.ShapeDtypeS...]
where the time goes in v3:
time: 46.4 us; the launch traced here: 46.2 us
  Pallas kernels  44.7 us (96%)
  local copies, waits for them, and re-layouts  1.57 us (3%)
    pallas_call x1, Pallas kernels, fused(): pl.pallas_call(functools.partial(kernel, S, C), out_shape=jax.ShapeDtypeS...  44.7 us
    unnamed x1, local copies, waits for them, and re-layouts  1.57 us

profile of v3, /device:TPU:0, one launch (start us, length us, event | category | flops | bytes accessed | tf_op | source)
XLA Modules:
  0.0 46.2 jit_solution(4431210089391931079)
XLA Ops:
  0.0 44.7 %shard_map.64 = bf16[128,512]{1,0:T(8,128)(2,1)} custom-call(bf16[128,512]{1,0:T(8,128)(2,1)} %in_ref.1, bf16[3,128,256]{2,1,0:T(8,128)(2,1)} %pw_ref.1, f32[3,3,128]{2,1,0:T(4,128)} %bitcast.2, f32[2,128]{1,0:T(2,128)} %bitcast.3, f32[2,128,512]{2,1,0:T(8,128)} %f_ref.1, bf16[128,256]{1,0:T(8,128)(2,1)} %ow_ref.1), custom_call_target="tpu_custom_call" | custom-call | tf_op jit(solution)/shard_map/pallas_call | solution.py:506
  44.7 1.6 %copy.8 = bf16[128,512]{1,0:T(8,128)(2,1)} copy(bf16[128,512]{1,0:T(8,128)(2,1)} %shard_map.64) | data formatting | bytes 262144
